TPU v7x, 32 devices: a whole 2x2x4 slice. The times are simulated.
32 devices in a mesh: grp: 2 (over x), obs: 16 (over z, y, core).
Axes of the slice: x: 2, y: 2, z: 4, core: 2. Of those that a mesh axis runs over, the one named last changes fastest.
Arguments:
- anomalies: bfloat16 [512, 16384], P(('grp', 'obs')), parts along dimension 0, may hold values from -6 to 6
- innovations: bfloat16 [512, 16384], P(('grp', 'obs')), parts along dimension 0, may hold values from -6 to 6
- sort_order: int32 [32768], P(('grp', 'obs')), parts along dimension 0, may hold values from 0 to 16383, as said below
- obs_error: float32 [32768], P(('grp', 'obs')), parts along dimension 0, may hold values from 0.2 to 2
Outputs:
- gain_product: float32 [32768, 256], P(('grp', 'obs')), parts along dimension 0
There are 2 independent parts, one for each index of `grp`. A program takes and returns all parts, laid end to end along the dimension named above; each array names one. Nothing has to cross between parts.
Inputs may be any that keep to these rules, and one draw needn't show every extreme that they name: Each acquisition index appears exactly once, and sort_order[p] lies in the same aligned block of 128 positions as p.
All inputs are finite; a program needn't handle non-finite values.
Results may differ from a plain program's by a relative error of at most 0.0025.
Values may be sent and summed in bfloat16 or wider, within the bound.
A program may use at most 64 MiB of HBM per device.

v0:
```python
import jax
import jax.numpy as jnp
from jax import lax
from jax.sharding import PartitionSpec as P


def shifted(shard, axis, by):
    peers = lax.axis_size(axis)
    pairs = [(i, i + by) for i in range(peers) if 0 <= i + by < peers]
    return lax.ppermute(shard, axis, pairs)


def gaspari(z):
    inner = z * z * (z * (z * (-0.25 * z + 0.5) + 0.625) - 5.0 / 3.0) + 1.0
    zs = jnp.maximum(z, 1.0)
    outer = (
        zs * zs * (zs * (zs * (zs / 12.0 - 0.5) + 0.625) + 5.0 / 3.0)
        - 5.0 * zs
        + 4.0
        - 2.0 / (3.0 * zs)
    )
    return jnp.where(z <= 1.0, inner, jnp.where(z < 2.0, outer, 0.0 * z))


def taper_scale(first_row, rows, cols, offset, half_width, members):
    row_ids = first_row + lax.iota(jnp.int32, rows)
    col_ids = lax.iota(jnp.int32, cols) + offset * cols
    dist = jnp.abs(row_ids[:, None] - col_ids[None, :]).astype(jnp.float32)
    return gaspari(dist / half_width) / (members - 1.0)


def permute_blocks(values, selector, width, blocks):
    shaped = values.reshape(values.shape[0], blocks, width)
    moved = jnp.einsum("mbi,bij->mbj", shaped, selector, preferred_element_type=jnp.float32)
    return moved.astype(jnp.bfloat16).reshape(values.shape[0], blocks * width)


def on_device(anomalies, innovations, sort_order, obs_error):
    raw_y, raw_d = (
        lax.all_to_all(anomalies, "obs", split_axis=1, concat_axis=0, tiled=True),
        lax.all_to_all(innovations, "obs", split_axis=1, concat_axis=0, tiled=True),
    )
    members = raw_y.shape[0]
    panel = raw_y.shape[1]
    width = min(128, panel)
    blocks = panel // width
    local_ids = (sort_order % width).reshape(blocks, width)
    selector = (lax.iota(jnp.int32, width)[None, :, None] == local_ids[:, None, :]).astype(
        jnp.bfloat16
    )
    y_here = permute_blocks(raw_y, selector, width, blocks)
    d_here = permute_blocks(raw_d, selector, width, blocks)
    block = min(512, panel)
    half_width = panel // 2 * 1.0

    def tile_rows(first, y_cols, offset):
        row_part = lax.slice_in_dim(y_here, first, first + block, axis=1)
        gram = lax.dot_general(
            row_part, y_cols, (((0,), (0,)), ((), ())), preferred_element_type=jnp.float32
        )
        return (gram * taper_scale(first, block, panel, offset, half_width, members * 1.0)).astype(
            jnp.bfloat16
        )

    def apply_rows(weights, d_cols):
        return lax.dot_general(
            weights, d_cols, (((1,), (1,)), ((), ())), preferred_element_type=jnp.float32
        )

    pieces = []
    low_y, low_d = shifted((y_here, d_here), "obs", 1)
    up_y, up_d = shifted((y_here, d_here), "obs", -1)
    for first in range(0, panel, block):
        acc = apply_rows(tile_rows(first, y_here, 0), d_here)
        acc = acc + apply_rows(tile_rows(first, low_y, -1), low_d)
        acc = acc + apply_rows(tile_rows(first, up_y, 1), up_d)
        pieces.append(acc)
    total = jnp.concatenate(pieces, axis=0)
    return total + obs_error[:, None] * d_here.T.astype(jnp.float32)


def solution(mesh):
    return jax.shard_map(
        on_device,
        mesh=mesh,
        in_specs=(
            P(("grp", "obs"), None),
            P(("grp", "obs"), None),
            P(("grp", "obs")),
            P(("grp", "obs")),
        ),
        out_specs=P(("grp", "obs"), None),
        check_vma=False,
    )
```

profile of v0, /device:TPU:1, one launch (start us, length us, event | category | flops | bytes accessed | tf_op | source)
XLA Modules:
  0.0 76.1 jit_solution(12527095984979136979)
XLA Ops:
  0.0 1.9 %copy.19 = bf16[2,16,8,1024]{3,2,0,1:T(8,128)(2,1)} copy(bf16[2,16,8,1024]{3,2,1,0:T(8,128)(2,1)} %bitcast.47) | data formatting | bytes 1048576 | tf_op jit(solution)/shard_map/all_to_all | solution.py:41
  1.9 7.3 %all-to-all-start.1 = ((bf16[16,16,1024]{2,0,1:T(8,128)(2,1)}), bf16[16,16,1024]{2,0,1:T(8,128)(2,1)S(1)}, u32[]{:S(2)}, u32[]{:S(2)}) async-start(bf16[16,16,1024]{2,0,1:T(8,128)(2,1)} %bitcast.37), calls=%async_computation.1 | async-start | bytes 1048576 | tf_op jit(solution)/shard_map/all_to_all | solution.py:41
  9.3 0.0 copy-start.2
  9.3 0.8 %copy.20 = bf16[2,16,8,1024]{3,2,0,1:T(8,128)(2,1)} copy(bf16[2,16,8,1024]{3,2,1,0:T(8,128)(2,1)S(1)} %bitcast.48) | data formatting | bytes 1048576 | tf_op jit(solution)/shard_map/all_to_all | solution.py:40
  10.1 13.2 %all-to-all-done.1 = bf16[16,16,1024]{2,0,1:T(8,128)(2,1)S(1)} async-done(((bf16[16,16,1024]{2,0,1:T(8,128)(2,1)}), bf16[16,16,1024]{2,0,1:T(8,128)(2,1)S(1)}, u32[]{:S(2)}, u32[]{:S(2)}) %all-to-all-start.1) | async-done | bytes 524320 | tf_op jit(solution)/shard_map/all_to_all | solution.py:41
  23.4 4.5 %all-to-all-start = ((bf16[16,16,1024]{2,0,1:T(8,128)(2,1)}), bf16[16,16,1024]{2,0,1:T(8,128)(2,1)S(1)}, u32[]{:S(2)}, u32[]{:S(2)}) async-start(bf16[16,16,1024]{2,0,1:T(8,128)(2,1)} %bitcast.38), calls=%async_computation | async-start | bytes 1048576 | tf_op jit(solution)/shard_map/all_to_all | solution.py:40
  27.9 0.1 copy.12
  28.0 0.3 convolution_convert_fusion
  28.4 3.5 %collective-permute-start.1 = (bf16[256,1024]{0,1:T(8,128)(2,1)S(1)}, bf16[256,1024]{0,1:T(8,128)(2,1)S(1)}, u32[]{:S(2)}, u32[]{:S(2)}) collective-permute-start(bf16[256,1024]{0,1:T(8,128)(2,1)S(1)} %bitcast.39), channel_id=1, source_target_pairs={{0,1},{1,2},{2,3},{3,4},{4,5},{5,6},{6,7},{7,8},{8,9},{9,10},{10,1... | collective-permute-start | bytes 1572872 | tf_op jit(solution)/shard_map/ppermute | solution.py:10
  31.9 1.9 %collective-permute-start.3 = (bf16[256,1024]{0,1:T(8,128)(2,1)S(1)}, bf16[256,1024]{0,1:T(8,128)(2,1)S(1)}, u32[]{:S(2)}, u32[]{:S(2)}) collective-permute-start(bf16[256,1024]{0,1:T(8,128)(2,1)S(1)} %bitcast.40), channel_id=1, source_target_pairs={{1,0},{2,1},{3,2},{4,3},{5,4},{6,5},{7,6},{8,7},{9,8},{10,9},{11,1... | collective-permute-start | bytes 1572872 | tf_op jit(solution)/shard_map/ppermute | solution.py:10
  33.8 8.1 %all-to-all-done = bf16[16,16,1024]{2,0,1:T(8,128)(2,1)S(1)} async-done(((bf16[16,16,1024]{2,0,1:T(8,128)(2,1)}), bf16[16,16,1024]{2,0,1:T(8,128)(2,1)S(1)}, u32[]{:S(2)}, u32[]{:S(2)}) %all-to-all-start) | async-done | bytes 524320 | tf_op jit(solution)/shard_map/all_to_all | solution.py:40
  41.9 0.1 copy.11
  42.0 0.3 convolution_convert_fusion.1
  42.4 2.5 %collective-permute-start = (bf16[256,1024]{0,1:T(8,128)(2,1)S(1)}, bf16[256,1024]{0,1:T(8,128)(2,1)S(1)}, u32[]{:S(2)}, u32[]{:S(2)}) collective-permute-start(bf16[256,1024]{0,1:T(8,128)(2,1)S(1)} %bitcast.49), channel_id=1, source_target_pairs={{0,1},{1,2},{2,3},{3,4},{4,5},{5,6},{6,7},{7,8},{8,9},{9,10},{10,1... | collective-permute-start | bytes 1572872 | tf_op jit(solution)/shard_map/ppermute | solution.py:10
  44.9 1.9 %collective-permute-start.2 = (bf16[256,1024]{0,1:T(8,128)(2,1)S(1)}, bf16[256,1024]{0,1:T(8,128)(2,1)}, u32[]{:S(2)}, u32[]{:S(2)}) collective-permute-start(bf16[256,1024]{0,1:T(8,128)(2,1)S(1)} %bitcast.50), channel_id=1, source_target_pairs={{1,0},{2,1},{3,2},{4,3},{5,4},{6,5},{7,6},{8,7},{9,8},{10,9},{11,1... | collective-permute-start | bytes 1572872 | tf_op jit(solution)/shard_map/ppermute | solution.py:10
  46.8 3.8 %fusion.7 = f32[512,256]{1,0:T(8,128)} fusion(bf16[256,1024]{0,1:T(8,128)(2,1)S(1)} %bitcast.41, bf16[256,1024]{0,1:T(8,128)(2,1)S(1)} %bitcast.51, s32[512]{0:T(512)S(1)} %iota_add_fusion.2), kind=kOutput, calls=%fused_computation.43 | convolution fusion | flops 555745280 | bytes 1837056 | tf_op jit(solution)/shard_map/dot_general | solution.py:66
  50.6 2.8 %fusion.6 = f32[512,256]{1,0:T(8,128)S(1)} fusion(bf16[256,1024]{0,1:T(8,128)(2,1)S(1)} %bitcast.42, bf16[256,1024]{0,1:T(8,128)(2,1)S(1)} %bitcast.52), kind=kOutput, calls=%fused_computation.42 | convolution fusion | flops 555745280 | bytes 1835008 | tf_op jit(solution)/shard_map/dot_general | solution.py:66
  53.3 0.0 collective-permute-done.1
  53.3 4.8 %collective-permute-done = bf16[256,1024]{0,1:T(8,128)(2,1)S(1)} collective-permute-done((bf16[256,1024]{0,1:T(8,128)(2,1)S(1)}, bf16[256,1024]{0,1:T(8,128)(2,1)S(1)}, u32[]{:S(2)}, u32[]{:S(2)}) %collective-permute-start) | collective-permute-done | bytes 524320 | tf_op jit(solution)/shard_map/ppermute | solution.py:10
  58.1 4.8 %convolution_add_fusion.1 = f32[512,256]{1,0:T(8,128)} fusion(f32[512,256]{1,0:T(8,128)} %fusion.7, bf16[256,1024]{0,1:T(8,128)(2,1)S(1)} %collective-permute-done.1, bf16[256,1024]{0,1:T(8,128)(2,1)S(1)} %collective-permute-done, s32[512]{0:T(512)S(1)} %iota_add_fusion.2, s32[1024]{0:T(1024)S(1)} %iota_add_fusion.1, bf16[256,1024]{0,1:T(8,128)(2,1)S(1)} %bitcast.53), kind=kOutput, calls=%fused_computation.39 | convolution fusion | flops 555876352 | bytes 2365440 | tf_op jit(solution)/shard_map/dot_general | solution.py:66
  62.9 3.7 %convolution_add_fusion.3 = f32[512,256]{1,0:T(8,128)} fusion(f32[512,256]{1,0:T(8,128)S(1)} %fusion.6, bf16[256,1024]{0,1:T(8,128)(2,1)S(1)} %collective-permute-done.1, bf16[256,1024]{0,1:T(8,128)(2,1)S(1)} %collective-permute-done, s32[1024]{0:T(1024)S(1)} %iota_add_fusion.1, bf16[256,1024]{0,1:T(8,128)(2,1)S(1)} %bitcast.54), kind=kOutput, calls=%fused_computation.41 | convolution fusion | flops 555876352 | bytes 2363392 | tf_op jit(solution)/shard_map/dot_general | solution.py:66
  66.6 4.4 %convolution_add_fusion = f32[512,256]{1,0:T(8,128)S(1)} fusion(f32[512,256]{1,0:T(8,128)} %convolution_add_fusion.1, bf16[256,1024]{0,1:T(8,128)(2,1)S(1)} %collective-permute-done.3, bf16[256,1024]{0,1:T(8,128)(2,1)} %collective-permute-done.2, s32[512]{0:T(512)S(1)} %iota_add_fusion.2, s32[1024]{0:T(1024)S(1)} %iota_add_fusion, ...), kind=kOutput, calls=%fused_computation.38 | convolution fusion | flops 555876352 | bytes 2365440 | tf_op jit(solution)/shard_map/dot_general | solution.py:66
  71.0 4.0 %convolution_add_fusion.2 = f32[512,256]{1,0:T(8,128)S(1)} fusion(f32[512,256]{1,0:T(8,128)S(1)} %copy-done.3, bf16[256,1024]{0,1:T(8,128)(2,1)S(1)} %collective-permute-done.3, bf16[256,1024]{0,1:T(8,128)(2,1)} %collective-permute-done.2, s32[1024]{0:T(1024)S(1)} %iota_add_fusion, bf16[256,1024]{0,1:T(8,128)(2,1)S(1)} %bitcast.56), kind=kOutput, calls=%fused_computation.40 | convolution fusion | flops 555876352 | bytes 2363392 | tf_op jit(solution)/shard_map/dot_general | solution.py:66
  75.0 1.2 %maximum_add_fusion = f32[1024,256]{1,0:T(8,128)} fusion(f32[512,256]{1,0:T(8,128)S(1)} %convolution_add_fusion, f32[512,256]{1,0:T(8,128)S(1)} %convolution_add_fusion.2, f32[1024]{0:T(1024)S(1)} %copy-done.1, bf16[8,128,256]{2,1,0:T(8,128)(2,1)S(1)} %convolution_convert_fusion), kind=kLoop, calls=%fused_computation.44 | loop fusion | flops 1048576 | bytes 2625536 | tf_op jit(solution)/shard_map/add | solution.py:79
  (13 shorter events, 0.0 us)
Async XLA Ops:
  0.0 9.3 %copy-start = (bf16[16,16384]{1,0:T(8,128)(2,1)S(1)}, bf16[16,16384]{1,0:T(8,128)(2,1)}, u32[]{:S(2)}) copy-start(bf16[16,16384]{1,0:T(8,128)(2,1)} %param.4) | copy-start | bytes 1572868
  1.9 21.4 %all-to-all-start.1 = ((bf16[16,16,1024]{2,0,1:T(8,128)(2,1)}), bf16[16,16,1024]{2,0,1:T(8,128)(2,1)S(1)}, u32[]{:S(2)}, u32[]{:S(2)}) async-start(bf16[16,16,1024]{2,0,1:T(8,128)(2,1)} %bitcast.37), calls=%async_computation.1 | async-start | bytes 1048576 | tf_op jit(solution)/shard_map/all_to_all | solution.py:41
  9.3 18.6 %copy-start.2 = (s32[1024]{0:T(1024)S(1)}, s32[1024]{0:T(1024)}, u32[]{:S(2)}) copy-start(s32[1024]{0:T(1024)} %param.6) | copy-start | bytes 12292
  23.4 18.6 %all-to-all-start = ((bf16[16,16,1024]{2,0,1:T(8,128)(2,1)}), bf16[16,16,1024]{2,0,1:T(8,128)(2,1)S(1)}, u32[]{:S(2)}, u32[]{:S(2)}) async-start(bf16[16,16,1024]{2,0,1:T(8,128)(2,1)} %bitcast.38), calls=%async_computation | async-start | bytes 1048576 | tf_op jit(solution)/shard_map/all_to_all | solution.py:40
  28.4 25.0 %collective-permute-start.1 = (bf16[256,1024]{0,1:T(8,128)(2,1)S(1)}, bf16[256,1024]{0,1:T(8,128)(2,1)S(1)}, u32[]{:S(2)}, u32[]{:S(2)}) collective-permute-start(bf16[256,1024]{0,1:T(8,128)(2,1)S(1)} %bitcast.39), channel_id=1, source_target_pairs={{0,1},{1,2},{2,3},{3,4},{4,5},{5,6},{6,7},{7,8},{8,9},{9,10},{10,1... | collective-permute-start | bytes 1572872 | tf_op jit(solution)/shard_map/ppermute | solution.py:10
  31.9 34.7 %collective-permute-start.3 = (bf16[256,1024]{0,1:T(8,128)(2,1)S(1)}, bf16[256,1024]{0,1:T(8,128)(2,1)S(1)}, u32[]{:S(2)}, u32[]{:S(2)}) collective-permute-start(bf16[256,1024]{0,1:T(8,128)(2,1)S(1)} %bitcast.40), channel_id=1, source_target_pairs={{1,0},{2,1},{3,2},{4,3},{5,4},{6,5},{7,6},{8,7},{9,8},{10,9},{11,1... | collective-permute-start | bytes 1572872 | tf_op jit(solution)/shard_map/ppermute | solution.py:10
  42.4 15.7 %collective-permute-start = (bf16[256,1024]{0,1:T(8,128)(2,1)S(1)}, bf16[256,1024]{0,1:T(8,128)(2,1)S(1)}, u32[]{:S(2)}, u32[]{:S(2)}) collective-permute-start(bf16[256,1024]{0,1:T(8,128)(2,1)S(1)} %bitcast.49), channel_id=1, source_target_pairs={{0,1},{1,2},{2,3},{3,4},{4,5},{5,6},{6,7},{7,8},{8,9},{9,10},{10,1... | collective-permute-start | bytes 1572872 | tf_op jit(solution)/shard_map/ppermute | solution.py:10
  44.9 21.7 %collective-permute-start.2 = (bf16[256,1024]{0,1:T(8,128)(2,1)S(1)}, bf16[256,1024]{0,1:T(8,128)(2,1)}, u32[]{:S(2)}, u32[]{:S(2)}) collective-permute-start(bf16[256,1024]{0,1:T(8,128)(2,1)S(1)} %bitcast.50), channel_id=1, source_target_pairs={{1,0},{2,1},{3,2},{4,3},{5,4},{6,5},{7,6},{8,7},{9,8},{10,9},{11,1... | collective-permute-start | bytes 1572872 | tf_op jit(solution)/shard_map/ppermute | solution.py:10
  66.6 4.4 %copy-start.3 = (f32[512,256]{1,0:T(8,128)S(1)}, f32[512,256]{1,0:T(8,128)}, u32[]{:S(2)}) copy-start(f32[512,256]{1,0:T(8,128)} %convolution_add_fusion.3) | copy-start | bytes 1572868
  71.0 4.0 %copy-start.1 = (f32[1024]{0:T(1024)S(1)}, f32[1024]{0:T(1024)}, u32[]{:S(2)}) copy-start(f32[1024]{0:T(1024)} %param.7) | copy-start | bytes 12292
where the time goes:
time: 76.6 us; the launch traced here: 76.1 us
  waiting for transfers between devices  26.1 us (34%)
  matrix products  24 us (31%)
  starting transfers between devices  21.7 us (28%)
  local copies, waits for them, and re-layouts  2.97 us (4%)
  other arithmetic  1.21 us (2%)
    dot_general x6, matrix products, apply_rows(): lax.dot_general(weights, d_cols, (((1,), (1,)), ((), ())), preferred_elem...  23.3 us
    all_to_all x1, waiting for transfers between devices, on_device(): lax.all_to_all(innovations, 'obs', split_axis=1, concat_axis=0, tiled=True)  13.2 us
    ppermute x4, starting transfers between devices, shifted(): return lax.ppermute(shard, axis, pairs)  9.9 us
    all_to_all x1, waiting for transfers between devices, on_device(): lax.all_to_all(anomalies, 'obs', split_axis=1, concat_axis=0, tiled=True)  8.09 us
    all_to_all x1, starting transfers between devices, on_device(): lax.all_to_all(innovations, 'obs', split_axis=1, concat_axis=0, tiled=True)  7.35 us
    ppermute x4, waiting for transfers between devices, shifted(): return lax.ppermute(shard, axis, pairs)  4.78 us
    all_to_all x1, starting transfers between devices, on_device(): lax.all_to_all(anomalies, 'obs', split_axis=1, concat_axis=0, tiled=True)  4.5 us
    all_to_all x1, local copies, waits for them, and re-layouts, on_device(): lax.all_to_all(innovations, 'obs', split_axis=1, concat_axis=0, tiled=True)  1.93 us
  transfers between devices with their start and end apart: 6, of which 3 were waited for; matrix products, arithmetic and copies ran while one was open for 22% of the time, Pallas kernels for 0%

commit v1 on v0

--- a/solution.py
+++ b/solution.py
@@ -2,6 +2,29 @@
 import jax.numpy as jnp
 from jax import lax
 from jax.sharding import PartitionSpec as P
+
+
+def cut_along(shard, dim, length):
+    dims = shard.shape
+    pieces = shard.reshape(*dims[:dim], length, dims[dim] // length, *dims[dim + 1 :])
+    return jnp.moveaxis(pieces, dim, 0)
+
+
+def laid_out(tiles, dim):
+    tiles = jnp.moveaxis(tiles, 0, dim)
+    shape = tiles.shape
+    return tiles.reshape(*shape[:dim], shape[dim] * shape[dim + 1], *shape[dim + 2 :])
+
+
+def pairwise_exchange(x, axis, split_dim, concat_dim):
+    devices, index = (lax.axis_size(axis), lax.axis_index(axis))
+    parts = cut_along(x, split_dim, devices)
+    gathered = [parts[index]]
+    for step in range(1, devices):
+        sent = parts[index ^ step]
+        gathered.append(lax.ppermute(sent, axis, [(i, i ^ step) for i in range(devices)]))
+    parts = jnp.stack(gathered)[index ^ jnp.arange(devices)]
+    return laid_out(parts, concat_dim)
 
 
 def shifted(shard, axis, by):
@@ -37,7 +60,7 @@
 
 def on_device(anomalies, innovations, sort_order, obs_error):
     raw_y, raw_d = (
-        lax.all_to_all(anomalies, "obs", split_axis=1, concat_axis=0, tiled=True),
+        pairwise_exchange(anomalies, "obs", 1, 0),
         lax.all_to_all(innovations, "obs", split_axis=1, concat_axis=0, tiled=True),
     )
     members = raw_y.shape[0]

time: 76.6 us -> 84.2 us (1.099)
  starting transfers between devices: 21.7 us -> 40.4 us
  waiting for transfers between devices: 26.1 us -> 11.4 us
  matrix products: 24 us -> 25.7 us
  local copies, waits for them, and re-layouts: 2.97 us -> 4.65 us
    ppermute x0 -> x15, starting transfers between devices: none -> 23 us  [pairwise_exchange(): lax.ppermute(sent, axis, [(i, i ^ step) for i in range(devices)])]
    all_to_all x1, waiting for transfers between devices: 13.2 us -> 0.01 us  [on_device(): lax.all_to_all(innovations, 'obs', split_axis=1, concat_axis=0, tiled=True)]
    all_to_all x1 -> x0, waiting for transfers between devices: 8.09 us -> none  [on_device(): lax.all_to_all(anomalies, 'obs', split_axis=1, concat_axis=0, tiled=True)]
    all_to_all x1 -> x0, starting transfers between devices: 4.5 us -> none  [on_device(): lax.all_to_all(anomalies, 'obs', split_axis=1, concat_axis=0, tiled=True)]
    ppermute x0 -> x15, waiting for transfers between devices: none -> 3.92 us  [pairwise_exchange(): lax.ppermute(sent, axis, [(i, i ^ step) for i in range(devices)])]
    ppermute x4, waiting for transfers between devices: 4.78 us -> 7.49 us  [shifted(): return lax.ppermute(shard, axis, pairs)]
    dot_general x6, matrix products: 23.3 us -> 25 us  [apply_rows(): lax.dot_general(weights, d_cols, (((1,), (1,)), ((), ())), preferred_elem...]
    another operation x0 -> x2, local copies, waits for them, and re-layouts: none -> 1.35 us
  transfers between devices with their start and end apart: 6 -> 20, of which waited for: 3 -> 4; matrix products, arithmetic and copies ran while one was open for 22% -> 24% of each run, Pallas kernels for 0% -> 0%
where the time goes in v1:
time: 84.2 us; the launch traced here: 83.8 us
  starting transfers between devices  40.4 us (48%)
  matrix products  25.7 us (31%)
  waiting for transfers between devices  11.4 us (14%)
  local copies, waits for them, and re-layouts  4.65 us (6%)
  other arithmetic  1.21 us (1%)
    dot_general x6, matrix products, apply_rows(): lax.dot_general(weights, d_cols, (((1,), (1,)), ((), ())), preferred_elem...  25 us
    ppermute x15, starting transfers between devices, pairwise_exchange(): lax.ppermute(sent, axis, [(i, i ^ step) for i in range(devices)])  23 us
    ppermute x4, starting transfers between devices, shifted(): return lax.ppermute(shard, axis, pairs)  10.1 us
    ppermute x4, waiting for transfers between devices, shifted(): return lax.ppermute(shard, axis, pairs)  7.49 us
    all_to_all x1, starting transfers between devices, on_device(): lax.all_to_all(innovations, 'obs', split_axis=1, concat_axis=0, tiled=True)  7.35 us
    ppermute x15, waiting for transfers between devices, pairwise_exchange(): lax.ppermute(sent, axis, [(i, i ^ step) for i in range(devices)])  3.92 us
    all_to_all x1, local copies, waits for them, and re-layouts, on_device(): lax.all_to_all(innovations, 'obs', split_axis=1, concat_axis=0, tiled=True)  1.93 us
  transfers between devices with their start and end apart: 20, of which 4 were waited for; matrix products, arithmetic and copies ran while one was open for 24% of the time, Pallas kernels for 0%

profile of v1, /device:TPU:1, one launch (start us, length us, event | category | flops | bytes accessed | tf_op | source)
XLA Modules:
  0.0 83.8 jit_solution(9657686872216921633)
XLA Ops:
  0.0 1.9 %copy.52 = bf16[2,16,8,1024]{3,2,0,1:T(8,128)(2,1)} copy(bf16[2,16,8,1024]{3,2,1,0:T(8,128)(2,1)} %bitcast.124) | data formatting | bytes 1048576 | tf_op jit(solution)/shard_map/all_to_all | solution.py:64
  1.9 7.3 %all-to-all-start = ((bf16[16,16,1024]{2,0,1:T(8,128)(2,1)}), bf16[16,16,1024]{2,0,1:T(8,128)(2,1)S(1)}, u32[]{:S(2)}, u32[]{:S(2)}) async-start(bf16[16,16,1024]{2,0,1:T(8,128)(2,1)} %bitcast.99), calls=%async_computation | async-start | bytes 1048576 | tf_op jit(solution)/shard_map/all_to_all | solution.py:64
  11.3 1.6 %collective-permute-start.1 = (bf16[16,1024]{1,0:T(8,128)(2,1)S(1)}, bf16[16,1024]{1,0:T(8,128)(2,1)S(1)}, u32[]{:S(2)}, u32[]{:S(2)}) collective-permute-start(bf16[16,1024]{1,0:T(8,128)(2,1)S(1)} %bitcast.147), channel_id=1, source_target_pairs={{0,2},{1,3},{2,0},{3,1},{4,6},{5,7},{6,4},{7,5},{8,10},{9,11},{10,... | collective-permute-start | bytes 98312 | tf_op jit(solution)/shard_map/ppermute | solution.py:25
  13.4 1.5 %collective-permute-start.3 = (bf16[16,1024]{1,0:T(8,128)(2,1)S(1)}, bf16[16,1024]{1,0:T(8,128)(2,1)S(1)}, u32[]{:S(2)}, u32[]{:S(2)}) collective-permute-start(bf16[16,1024]{1,0:T(8,128)(2,1)S(1)} %bitcast.144), channel_id=1, source_target_pairs={{0,4},{1,5},{2,6},{3,7},{4,0},{5,1},{6,2},{7,3},{8,12},{9,13},{10,... | collective-permute-start | bytes 98312 | tf_op jit(solution)/shard_map/ppermute | solution.py:25
  15.6 2.4 %collective-permute-start.5 = (bf16[16,1024]{1,0:T(8,128)(2,1)S(1)}, bf16[16,1024]{1,0:T(8,128)(2,1)S(1)}, u32[]{:S(2)}, u32[]{:S(2)}) collective-permute-start(bf16[16,1024]{1,0:T(8,128)(2,1)S(1)} %bitcast.145), channel_id=1, source_target_pairs={{0,6},{1,7},{2,4},{3,5},{4,2},{5,3},{6,0},{7,1},{8,14},{9,15},{10,... | collective-permute-start | bytes 98312 | tf_op jit(solution)/shard_map/ppermute | solution.py:25
  18.0 1.6 %collective-permute-start.6 = (bf16[16,1024]{1,0:T(8,128)(2,1)S(1)}, bf16[16,1024]{1,0:T(8,128)(2,1)S(1)}, u32[]{:S(2)}, u32[]{:S(2)}) collective-permute-start(bf16[16,1024]{1,0:T(8,128)(2,1)S(1)} %bitcast.142), channel_id=1, source_target_pairs={{0,7},{1,6},{2,5},{3,4},{4,3},{5,2},{6,1},{7,0},{8,15},{9,14},{10,... | collective-permute-start | bytes 98312 | tf_op jit(solution)/shard_map/ppermute | solution.py:25
  19.6 1.5 %collective-permute-start.7 = (bf16[16,1024]{1,0:T(8,128)(2,1)S(1)}, bf16[16,1024]{1,0:T(8,128)(2,1)S(1)}, u32[]{:S(2)}, u32[]{:S(2)}) collective-permute-start(bf16[16,1024]{1,0:T(8,128)(2,1)S(1)} %bitcast.141), channel_id=1, source_target_pairs={{0,8},{1,9},{2,10},{3,11},{4,12},{5,13},{6,14},{7,15},{8,0},{9,1},... | collective-permute-start | bytes 98312 | tf_op jit(solution)/shard_map/ppermute | solution.py:25
  21.1 3.1 %collective-permute-start.8 = (bf16[16,1024]{1,0:T(8,128)(2,1)S(1)}, bf16[16,1024]{1,0:T(8,128)(2,1)S(1)}, u32[]{:S(2)}, u32[]{:S(2)}) collective-permute-start(bf16[16,1024]{1,0:T(8,128)(2,1)S(1)} %bitcast.140), channel_id=1, source_target_pairs={{0,9},{1,8},{2,11},{3,10},{4,13},{5,12},{6,15},{7,14},{8,1},{9,0},... | collective-permute-start | bytes 98312 | tf_op jit(solution)/shard_map/ppermute | solution.py:25
  27.8 3.5 %collective-permute-start.12 = (bf16[16,1024]{1,0:T(8,128)(2,1)S(1)}, bf16[16,1024]{1,0:T(8,128)(2,1)S(1)}, u32[]{:S(2)}, u32[]{:S(2)}) collective-permute-start(bf16[16,1024]{1,0:T(8,128)(2,1)S(1)} %bitcast.136), channel_id=1, source_target_pairs={{0,13},{1,12},{2,15},{3,14},{4,9},{5,8},{6,11},{7,10},{8,5},{9,4},... | collective-permute-start | bytes 98312 | tf_op jit(solution)/shard_map/ppermute | solution.py:25
  32.4 2.1 %collective-permute-start.14 = (bf16[16,1024]{1,0:T(8,128)(2,1)S(1)}, bf16[16,1024]{1,0:T(8,128)(2,1)S(1)}, u32[]{:S(2)}, u32[]{:S(2)}) collective-permute-start(bf16[16,1024]{1,0:T(8,128)(2,1)S(1)} %bitcast.134), channel_id=1, source_target_pairs={{0,15},{1,14},{2,13},{3,12},{4,11},{5,10},{6,9},{7,8},{8,7},{9,6},... | collective-permute-start | bytes 98312 | tf_op jit(solution)/shard_map/ppermute | solution.py:25
  34.6 2.2 %collective-permute-done.13 = bf16[16,1024]{1,0:T(8,128)(2,1)S(1)} collective-permute-done((bf16[16,1024]{1,0:T(8,128)(2,1)S(1)}, bf16[16,1024]{1,0:T(8,128)(2,1)S(1)}, u32[]{:S(2)}, u32[]{:S(2)}) %collective-permute-start.13) | collective-permute-done | bytes 32800 | tf_op jit(solution)/shard_map/ppermute | solution.py:25
  36.8 1.7 %collective-permute-done.14 = bf16[16,1024]{1,0:T(8,128)(2,1)S(1)} collective-permute-done((bf16[16,1024]{1,0:T(8,128)(2,1)S(1)}, bf16[16,1024]{1,0:T(8,128)(2,1)S(1)}, u32[]{:S(2)}, u32[]{:S(2)}) %collective-permute-start.14) | collective-permute-done | bytes 32800 | tf_op jit(solution)/shard_map/ppermute | solution.py:25
  39.5 2.4 %collective-permute-start.15 = (bf16[256,1024]{0,1:T(8,128)(2,1)S(1)}, bf16[256,1024]{0,1:T(8,128)(2,1)S(1)}, u32[]{:S(2)}, u32[]{:S(2)}) collective-permute-start(bf16[256,1024]{0,1:T(8,128)(2,1)S(1)} %bitcast.126), channel_id=1, source_target_pairs={{0,1},{1,2},{2,3},{3,4},{4,5},{5,6},{6,7},{7,8},{8,9},{9,10},{10,1... | collective-permute-start | bytes 1572872 | tf_op jit(solution)/shard_map/ppermute | solution.py:33
  41.9 1.9 %collective-permute-start.17 = (bf16[256,1024]{0,1:T(8,128)(2,1)S(1)}, bf16[256,1024]{0,1:T(8,128)(2,1)S(1)}, u32[]{:S(2)}, u32[]{:S(2)}) collective-permute-start(bf16[256,1024]{0,1:T(8,128)(2,1)S(1)} %bitcast.127), channel_id=1, source_target_pairs={{1,0},{2,1},{3,2},{4,3},{5,4},{6,5},{7,6},{8,7},{9,8},{10,9},{11,1... | collective-permute-start | bytes 1572872 | tf_op jit(solution)/shard_map/ppermute | solution.py:33
  44.4 3.6 %collective-permute-start.16 = (bf16[256,1024]{0,1:T(8,128)(2,1)S(1)}, bf16[256,1024]{0,1:T(8,128)(2,1)S(1)}, u32[]{:S(2)}, u32[]{:S(2)}) collective-permute-start(bf16[256,1024]{0,1:T(8,128)(2,1)S(1)} %bitcast.116), channel_id=1, source_target_pairs={{0,1},{1,2},{2,3},{3,4},{4,5},{5,6},{6,7},{7,8},{8,9},{9,10},{10,1... | collective-permute-start | bytes 1572872 | tf_op jit(solution)/shard_map/ppermute | solution.py:33
  48.0 2.1 %collective-permute-start.18 = (bf16[256,1024]{0,1:T(8,128)(2,1)S(1)}, bf16[256,1024]{0,1:T(8,128)(2,1)S(1)}, u32[]{:S(2)}, u32[]{:S(2)}) collective-permute-start(bf16[256,1024]{0,1:T(8,128)(2,1)S(1)} %bitcast.117), channel_id=1, source_target_pairs={{1,0},{2,1},{3,2},{4,3},{5,4},{6,5},{7,6},{8,7},{9,8},{10,9},{11,1... | collective-permute-start | bytes 1572872 | tf_op jit(solution)/shard_map/ppermute | solution.py:33
  50.1 3.8 %fusion.7 = f32[512,256]{1,0:T(8,128)} fusion(bf16[256,1024]{0,1:T(8,128)(2,1)S(1)} %bitcast.118, bf16[256,1024]{0,1:T(8,128)(2,1)S(1)} %bitcast.128, s32[512]{0:T(512)S(1)} %iota_add_fusion.2), kind=kOutput, calls=%fused_computation.44 | convolution fusion | flops 555745280 | bytes 1837056 | tf_op jit(solution)/shard_map/dot_general | solution.py:89
  53.8 3.6 %fusion.6 = f32[512,256]{1,0:T(8,128)} fusion(bf16[256,1024]{0,1:T(8,128)(2,1)S(1)} %bitcast.119, bf16[256,1024]{0,1:T(8,128)(2,1)S(1)} %bitcast.129), kind=kOutput, calls=%fused_computation.43 | convolution fusion | flops 555745280 | bytes 1835008 | tf_op jit(solution)/shard_map/dot_general | solution.py:89
  57.4 1.9 %collective-permute-done.15 = bf16[256,1024]{0,1:T(8,128)(2,1)S(1)} collective-permute-done((bf16[256,1024]{0,1:T(8,128)(2,1)S(1)}, bf16[256,1024]{0,1:T(8,128)(2,1)S(1)}, u32[]{:S(2)}, u32[]{:S(2)}) %collective-permute-start.15) | collective-permute-done | bytes 524320 | tf_op jit(solution)/shard_map/ppermute | solution.py:33
  59.3 5.6 %collective-permute-done.16 = bf16[256,1024]{0,1:T(8,128)(2,1)S(1)} collective-permute-done((bf16[256,1024]{0,1:T(8,128)(2,1)S(1)}, bf16[256,1024]{0,1:T(8,128)(2,1)S(1)}, u32[]{:S(2)}, u32[]{:S(2)}) %collective-permute-start.16) | collective-permute-done | bytes 524320 | tf_op jit(solution)/shard_map/ppermute | solution.py:33
  64.9 4.8 %convolution_add_fusion.1 = f32[512,256]{1,0:T(8,128)} fusion(f32[512,256]{1,0:T(8,128)} %fusion.7, bf16[256,1024]{0,1:T(8,128)(2,1)S(1)} %collective-permute-done.16, bf16[256,1024]{0,1:T(8,128)(2,1)S(1)} %collective-permute-done.15, s32[512]{0:T(512)S(1)} %iota_add_fusion.2, s32[1024]{0:T(1024)S(1)} %iota_add_fusion.1, bf16[256,1024]{0,1:T(8,128)(2,1)S(1)} %bitcast.130), kind=kOutput, calls=%fused_computation.40 | convolution fusion | flops 555876352 | bytes 2365440 | tf_op jit(solution)/shard_map/dot_general | solution.py:89
  69.7 4.8 %convolution_add_fusion.3 = f32[512,256]{1,0:T(8,128)} fusion(f32[512,256]{1,0:T(8,128)} %fusion.6, bf16[256,1024]{0,1:T(8,128)(2,1)S(1)} %collective-permute-done.16, bf16[256,1024]{0,1:T(8,128)(2,1)S(1)} %collective-permute-done.15, s32[1024]{0:T(1024)S(1)} %iota_add_fusion.1, bf16[256,1024]{0,1:T(8,128)(2,1)S(1)} %bitcast.131), kind=kOutput, calls=%fused_computation.42 | convolution fusion | flops 555876352 | bytes 2363392 | tf_op jit(solution)/shard_map/dot_general | solution.py:89
  74.4 4.2 %convolution_add_fusion = f32[512,256]{1,0:T(8,128)S(1)} fusion(f32[512,256]{1,0:T(8,128)} %convolution_add_fusion.1, bf16[256,1024]{0,1:T(8,128)(2,1)S(1)} %collective-permute-done.18, bf16[256,1024]{0,1:T(8,128)(2,1)S(1)} %collective-permute-done.17, s32[512]{0:T(512)S(1)} %iota_add_fusion.2, s32[1024]{0:T(1024)S(1)} %iota_add_fusion, ...), kind=kOutput, calls=%fused_computation.39 | convolution fusion | flops 555876352 | bytes 2365440 | tf_op jit(solution)/shard_map/dot_general | solution.py:89
  78.6 4.0 %convolution_add_fusion.2 = f32[512,256]{1,0:T(8,128)S(1)} fusion(f32[512,256]{1,0:T(8,128)} %convolution_add_fusion.3, bf16[256,1024]{0,1:T(8,128)(2,1)S(1)} %collective-permute-done.18, bf16[256,1024]{0,1:T(8,128)(2,1)S(1)} %collective-permute-done.17, s32[1024]{0:T(1024)S(1)} %iota_add_fusion, bf16[256,1024]{0,1:T(8,128)(2,1)S(1)} %bitcast.133), kind=kOutput, calls=%fused_computation.41 | convolution fusion | flops 555876352 | bytes 2363392 | tf_op jit(solution)/shard_map/dot_general | solution.py:89
  (74 shorter events, 10.4 us)
Async XLA Ops:
  0.0 9.3 %copy-start = (bf16[16,16384]{1,0:T(8,128)(2,1)S(1)}, bf16[16,16384]{1,0:T(8,128)(2,1)}, u32[]{:S(2)}) copy-start(bf16[16,16384]{1,0:T(8,128)(2,1)} %param.4) | copy-start | bytes 1572868
  1.9 42.0 %all-to-all-start = ((bf16[16,16,1024]{2,0,1:T(8,128)(2,1)}), bf16[16,16,1024]{2,0,1:T(8,128)(2,1)S(1)}, u32[]{:S(2)}, u32[]{:S(2)}) async-start(bf16[16,16,1024]{2,0,1:T(8,128)(2,1)} %bitcast.99), calls=%async_computation | async-start | bytes 1048576 | tf_op jit(solution)/shard_map/all_to_all | solution.py:64
  9.7 5.6 %copy-start.2 = (s32[1024]{0:T(1024)S(1)}, s32[1024]{0:T(1024)}, u32[]{:S(2)}) copy-start(s32[1024]{0:T(1024)} %param.6) | copy-start | bytes 12292
  11.1 4.5 %collective-permute-start = (bf16[16,1024]{1,0:T(8,128)(2,1)S(1)}, bf16[16,1024]{1,0:T(8,128)(2,1)S(1)}, u32[]{:S(2)}, u32[]{:S(2)}) collective-permute-start(bf16[16,1024]{1,0:T(8,128)(2,1)S(1)} %bitcast.148), channel_id=1, source_target_pairs={{0,1},{1,0},{2,3},{3,2},{4,5},{5,4},{6,7},{7,6},{8,9},{9,8},{10,11... | collective-permute-start | bytes 98312 | tf_op jit(solution)/shard_map/ppermute | solution.py:25
  11.3 6.7 %collective-permute-start.1 = (bf16[16,1024]{1,0:T(8,128)(2,1)S(1)}, bf16[16,1024]{1,0:T(8,128)(2,1)S(1)}, u32[]{:S(2)}, u32[]{:S(2)}) collective-permute-start(bf16[16,1024]{1,0:T(8,128)(2,1)S(1)} %bitcast.147), channel_id=1, source_target_pairs={{0,2},{1,3},{2,0},{3,1},{4,6},{5,7},{6,4},{7,5},{8,10},{9,11},{10,... | collective-permute-start | bytes 98312 | tf_op jit(solution)/shard_map/ppermute | solution.py:25
  13.0 6.6 %collective-permute-start.2 = (bf16[16,1024]{1,0:T(8,128)(2,1)S(1)}, bf16[16,1024]{1,0:T(8,128)(2,1)S(1)}, u32[]{:S(2)}, u32[]{:S(2)}) collective-permute-start(bf16[16,1024]{1,0:T(8,128)(2,1)S(1)} %bitcast.146), channel_id=1, source_target_pairs={{0,3},{1,2},{2,1},{3,0},{4,7},{5,6},{6,5},{7,4},{8,11},{9,10},{10,... | collective-permute-start | bytes 98312 | tf_op jit(solution)/shard_map/ppermute | solution.py:25
  13.4 7.7 %collective-permute-start.3 = (bf16[16,1024]{1,0:T(8,128)(2,1)S(1)}, bf16[16,1024]{1,0:T(8,128)(2,1)S(1)}, u32[]{:S(2)}, u32[]{:S(2)}) collective-permute-start(bf16[16,1024]{1,0:T(8,128)(2,1)S(1)} %bitcast.144), channel_id=1, source_target_pairs={{0,4},{1,5},{2,6},{3,7},{4,0},{5,1},{6,2},{7,3},{8,12},{9,13},{10,... | collective-permute-start | bytes 98312 | tf_op jit(solution)/shard_map/ppermute | solution.py:25
  14.9 9.3 %collective-permute-start.4 = (bf16[16,1024]{1,0:T(8,128)(2,1)S(1)}, bf16[16,1024]{1,0:T(8,128)(2,1)S(1)}, u32[]{:S(2)}, u32[]{:S(2)}) collective-permute-start(bf16[16,1024]{1,0:T(8,128)(2,1)S(1)} %bitcast.143), channel_id=1, source_target_pairs={{0,5},{1,4},{2,7},{3,6},{4,1},{5,0},{6,3},{7,2},{8,13},{9,12},{10,... | collective-permute-start | bytes 98312 | tf_op jit(solution)/shard_map/ppermute | solution.py:25
  15.6 9.9 %collective-permute-start.5 = (bf16[16,1024]{1,0:T(8,128)(2,1)S(1)}, bf16[16,1024]{1,0:T(8,128)(2,1)S(1)}, u32[]{:S(2)}, u32[]{:S(2)}) collective-permute-start(bf16[16,1024]{1,0:T(8,128)(2,1)S(1)} %bitcast.145), channel_id=1, source_target_pairs={{0,6},{1,7},{2,4},{3,5},{4,2},{5,3},{6,0},{7,1},{8,14},{9,15},{10,... | collective-permute-start | bytes 98312 | tf_op jit(solution)/shard_map/ppermute | solution.py:25
  18.0 8.5 %collective-permute-start.6 = (bf16[16,1024]{1,0:T(8,128)(2,1)S(1)}, bf16[16,1024]{1,0:T(8,128)(2,1)S(1)}, u32[]{:S(2)}, u32[]{:S(2)}) collective-permute-start(bf16[16,1024]{1,0:T(8,128)(2,1)S(1)} %bitcast.142), channel_id=1, source_target_pairs={{0,7},{1,6},{2,5},{3,4},{4,3},{5,2},{6,1},{7,0},{8,15},{9,14},{10,... | collective-permute-start | bytes 98312 | tf_op jit(solution)/shard_map/ppermute | solution.py:25
  19.6 8.2 %collective-permute-start.7 = (bf16[16,1024]{1,0:T(8,128)(2,1)S(1)}, bf16[16,1024]{1,0:T(8,128)(2,1)S(1)}, u32[]{:S(2)}, u32[]{:S(2)}) collective-permute-start(bf16[16,1024]{1,0:T(8,128)(2,1)S(1)} %bitcast.141), channel_id=1, source_target_pairs={{0,8},{1,9},{2,10},{3,11},{4,12},{5,13},{6,14},{7,15},{8,0},{9,1},... | collective-permute-start | bytes 98312 | tf_op jit(solution)/shard_map/ppermute | solution.py:25
  21.1 10.2 %collective-permute-start.8 = (bf16[16,1024]{1,0:T(8,128)(2,1)S(1)}, bf16[16,1024]{1,0:T(8,128)(2,1)S(1)}, u32[]{:S(2)}, u32[]{:S(2)}) collective-permute-start(bf16[16,1024]{1,0:T(8,128)(2,1)S(1)} %bitcast.140), channel_id=1, source_target_pairs={{0,9},{1,8},{2,11},{3,10},{4,13},{5,12},{6,15},{7,14},{8,1},{9,0},... | collective-permute-start | bytes 98312 | tf_op jit(solution)/shard_map/ppermute | solution.py:25
  24.2 8.2 %collective-permute-start.9 = (bf16[16,1024]{1,0:T(8,128)(2,1)S(1)}, bf16[16,1024]{1,0:T(8,128)(2,1)S(1)}, u32[]{:S(2)}, u32[]{:S(2)}) collective-permute-start(bf16[16,1024]{1,0:T(8,128)(2,1)S(1)} %bitcast.139), channel_id=1, source_target_pairs={{0,10},{1,11},{2,8},{3,9},{4,14},{5,15},{6,12},{7,13},{8,2},{9,3},... | collective-permute-start | bytes 98312 | tf_op jit(solution)/shard_map/ppermute | solution.py:25
  25.5 9.0 %collective-permute-start.10 = (bf16[16,1024]{1,0:T(8,128)(2,1)S(1)}, bf16[16,1024]{1,0:T(8,128)(2,1)S(1)}, u32[]{:S(2)}, u32[]{:S(2)}) collective-permute-start(bf16[16,1024]{1,0:T(8,128)(2,1)S(1)} %bitcast.138), channel_id=1, source_target_pairs={{0,11},{1,10},{2,9},{3,8},{4,15},{5,14},{6,13},{7,12},{8,3},{9,2},... | collective-permute-start | bytes 98312 | tf_op jit(solution)/shard_map/ppermute | solution.py:25
  26.5 8.0 %collective-permute-start.11 = (bf16[16,1024]{1,0:T(8,128)(2,1)S(1)}, bf16[16,1024]{1,0:T(8,128)(2,1)S(1)}, u32[]{:S(2)}, u32[]{:S(2)}) collective-permute-start(bf16[16,1024]{1,0:T(8,128)(2,1)S(1)} %bitcast.137), channel_id=1, source_target_pairs={{0,12},{1,13},{2,14},{3,15},{4,8},{5,9},{6,10},{7,11},{8,4},{9,5},... | collective-permute-start | bytes 98312 | tf_op jit(solution)/shard_map/ppermute | solution.py:25
  27.8 6.8 %collective-permute-start.12 = (bf16[16,1024]{1,0:T(8,128)(2,1)S(1)}, bf16[16,1024]{1,0:T(8,128)(2,1)S(1)}, u32[]{:S(2)}, u32[]{:S(2)}) collective-permute-start(bf16[16,1024]{1,0:T(8,128)(2,1)S(1)} %bitcast.136), channel_id=1, source_target_pairs={{0,13},{1,12},{2,15},{3,14},{4,9},{5,8},{6,11},{7,10},{8,5},{9,4},... | collective-permute-start | bytes 98312 | tf_op jit(solution)/shard_map/ppermute | solution.py:25
  31.3 5.5 %collective-permute-start.13 = (bf16[16,1024]{1,0:T(8,128)(2,1)S(1)}, bf16[16,1024]{1,0:T(8,128)(2,1)S(1)}, u32[]{:S(2)}, u32[]{:S(2)}) collective-permute-start(bf16[16,1024]{1,0:T(8,128)(2,1)S(1)} %bitcast.135), channel_id=1, source_target_pairs={{0,14},{1,15},{2,12},{3,13},{4,10},{5,11},{6,8},{7,9},{8,6},{9,7},... | collective-permute-start | bytes 98312 | tf_op jit(solution)/shard_map/ppermute | solution.py:25
  32.4 6.0 %collective-permute-start.14 = (bf16[16,1024]{1,0:T(8,128)(2,1)S(1)}, bf16[16,1024]{1,0:T(8,128)(2,1)S(1)}, u32[]{:S(2)}, u32[]{:S(2)}) collective-permute-start(bf16[16,1024]{1,0:T(8,128)(2,1)S(1)} %bitcast.134), channel_id=1, source_target_pairs={{0,15},{1,14},{2,13},{3,12},{4,11},{5,10},{6,9},{7,8},{8,7},{9,6},... | collective-permute-start | bytes 98312 | tf_op jit(solution)/shard_map/ppermute | solution.py:25
  39.5 19.8 %collective-permute-start.15 = (bf16[256,1024]{0,1:T(8,128)(2,1)S(1)}, bf16[256,1024]{0,1:T(8,128)(2,1)S(1)}, u32[]{:S(2)}, u32[]{:S(2)}) collective-permute-start(bf16[256,1024]{0,1:T(8,128)(2,1)S(1)} %bitcast.126), channel_id=1, source_target_pairs={{0,1},{1,2},{2,3},{3,4},{4,5},{5,6},{6,7},{7,8},{8,9},{9,10},{10,1... | collective-permute-start | bytes 1572872 | tf_op jit(solution)/shard_map/ppermute | solution.py:33
  41.9 32.5 %collective-permute-start.17 = (bf16[256,1024]{0,1:T(8,128)(2,1)S(1)}, bf16[256,1024]{0,1:T(8,128)(2,1)S(1)}, u32[]{:S(2)}, u32[]{:S(2)}) collective-permute-start(bf16[256,1024]{0,1:T(8,128)(2,1)S(1)} %bitcast.127), channel_id=1, source_target_pairs={{1,0},{2,1},{3,2},{4,3},{5,4},{6,5},{7,6},{8,7},{9,8},{10,9},{11,1... | collective-permute-start | bytes 1572872 | tf_op jit(solution)/shard_map/ppermute | solution.py:33
  44.4 20.5 %collective-permute-start.16 = (bf16[256,1024]{0,1:T(8,128)(2,1)S(1)}, bf16[256,1024]{0,1:T(8,128)(2,1)S(1)}, u32[]{:S(2)}, u32[]{:S(2)}) collective-permute-start(bf16[256,1024]{0,1:T(8,128)(2,1)S(1)} %bitcast.116), channel_id=1, source_target_pairs={{0,1},{1,2},{2,3},{3,4},{4,5},{5,6},{6,7},{7,8},{8,9},{9,10},{10,1... | collective-permute-start | bytes 1572872 | tf_op jit(solution)/shard_map/ppermute | solution.py:33
  48.0 26.5 %collective-permute-start.18 = (bf16[256,1024]{0,1:T(8,128)(2,1)S(1)}, bf16[256,1024]{0,1:T(8,128)(2,1)S(1)}, u32[]{:S(2)}, u32[]{:S(2)}) collective-permute-start(bf16[256,1024]{0,1:T(8,128)(2,1)S(1)} %bitcast.117), channel_id=1, source_target_pairs={{1,0},{2,1},{3,2},{4,3},{5,4},{6,5},{7,6},{8,7},{9,8},{10,9},{11,1... | collective-permute-start | bytes 1572872 | tf_op jit(solution)/shard_map/ppermute | solution.py:33
  78.6 4.0 %copy-start.1 = (f32[1024]{0:T(1024)S(1)}, f32[1024]{0:T(1024)}, u32[]{:S(2)}) copy-start(f32[1024]{0:T(1024)} %param.7) | copy-start | bytes 12292
